TPU v7x, 32 devices: a whole 2x2x4 slice. The times are simulated.
32 devices in a mesh: graph: 2 (over core), dom: 16 (over z, y, x).
Axes of the slice: x: 2, y: 2, z: 4, core: 2. Of those that a mesh axis runs over, the one named last changes fastest.
Arguments:
- embeddings: float32 [2, 8192, 300], P('graph', 'dom'), may hold values from -6 to 6
- first_weight: float32 [300, 300], replicated, may hold values from -0.375 to 0.375
- second_weight: float32 [300, 300], replicated, may hold values from -0.375 to 0.375
- bound_index: int32 [2, 16, 2, 64], P('graph', 'dom'), may hold values from 0 to 511
- neighbors: int32 [2, 8192, 16], P('graph', 'dom'), may hold values from 0 to 639
- degree: int32 [2, 8192], P('graph', 'dom'), may hold values from 1 to 16
- send_index: int32 [2, 16, 32, 32], P('graph', 'dom'), may hold values from 0 to 512, as said below
- recv_count: int32 [2, 16, 32], P('graph', 'dom'), may hold values from 8 to 32, as said below
- pair_index: int32 [2, 16, 2, 128], P('graph', 'dom'), may hold values from 0 to 1023, as said below
Outputs:
- grad_embeddings: float32 [2, 8192, 300], P('graph', 'dom')
- grad_first: float32 [300, 300], replicated
- grad_second: float32 [300, 300], replicated
- cluster_loss: float32 [2, 16], P('graph', 'dom')
Inputs may be any that keep to these rules, and one draw needn't show every extreme that they name: `send_index`: for each sending partition and owner, filled slots come first and hold local rows, the empty ones hold 512; every local row is sent exactly once; in each aligned group of four owners one receives 32 rows from every partition. `recv_count`: equals the number of filled slots that send_index gives for this owner and that partition. `pair_index`: entries are s * 32 + c. Side 0 names each of the first 8 slots of every graph-0 partition once, side 1 each of the first 8 slots of every graph-1 partition once.
All inputs are finite; a program needn't handle non-finite values.
Results may differ from a plain program's by a relative error of at most 0.0003.
Values sent between devices are 32-bit elements; how exact they have to be, the bound alone decides.
A program may use at most 64 MiB of HBM per device.

v0:
```python
import math
import jax
import jax.numpy as jnp
from jax import lax
from jax.sharding import PartitionSpec as P

SOFTMAX_HEAT = 0.02
EPSILON = 1e-06
TOP_PRECISION = lax.Precision.HIGHEST


def with_halo(cells, sides, width):
    for axis, dim in sides:
        count = lax.axis_size(axis)
        head = lax.slice_in_dim(cells, 0, width, axis=dim)
        tail = lax.slice_in_dim(cells, cells.shape[dim] - width, cells.shape[dim], axis=dim)
        cells = jnp.concatenate(
            [
                lax.ppermute(tail, axis, [(i, (i + 1) % count) for i in range(count)]),
                cells,
                lax.ppermute(head, axis, [((i + 1) % count, i) for i in range(count)]),
            ],
            axis=dim,
        )
    return cells


def count_matrix(pool_rows, neighbor_ids, degree_row):
    row_count = neighbor_ids.shape[0]
    rim_width = (pool_rows - row_count) // 2
    columns = jnp.arange(pool_rows, dtype=jnp.int32)
    slot_ids = jnp.arange(neighbor_ids.shape[1], dtype=jnp.int32)
    live_mask = slot_ids[None, :] < degree_row[:, None]
    hits = (neighbor_ids[:, :, None] == columns[None, None, :]) & live_mask[:, :, None]
    counts = jnp.sum(hits.astype(jnp.float32), axis=1)
    self_rows = jnp.arange(row_count, dtype=jnp.int32) + rim_width
    return counts + (columns[None, :] == self_rows[:, None]).astype(jnp.float32)


def aggregate(counts, pool, degree_row):
    summed = jnp.dot(counts, pool, precision=TOP_PRECISION, preferred_element_type=jnp.float32)
    return summed / (1.0 + degree_row.astype(jnp.float32))[:, None]


def cluster_term(incoming_rows, counts, pair_rows):
    slot_total = incoming_rows.shape[0]
    slot_cap = slot_total // counts.shape[0]
    live_mask = (jnp.arange(slot_cap, dtype=jnp.int32)[None, :] < counts[:, None]).reshape(
        slot_total
    )
    half_slot_count = slot_total // 2
    source_entity = incoming_rows[pair_rows[0]]
    target_entity = incoming_rows[pair_rows[1]]
    first_layer_logits = (
        jnp.dot(
            source_entity,
            incoming_rows[half_slot_count:].T,
            precision=TOP_PRECISION,
            preferred_element_type=jnp.float32,
        )
        / SOFTMAX_HEAT
    )
    second_layer_logits = (
        jnp.dot(
            target_entity,
            incoming_rows[:half_slot_count].T,
            precision=TOP_PRECISION,
            preferred_element_type=jnp.float32,
        )
        / SOFTMAX_HEAT
    )
    first_total = jnp.log(
        jnp.sum(
            jnp.where(live_mask[half_slot_count:][None, :], jnp.exp(first_layer_logits), 0.0),
            axis=1,
        )
    )
    second_total = jnp.log(
        jnp.sum(
            jnp.where(live_mask[:half_slot_count][None, :], jnp.exp(second_layer_logits), 0.0),
            axis=1,
        )
    )
    positive_match = jnp.sum(source_entity * target_entity, axis=1) / SOFTMAX_HEAT
    return jnp.sum(first_total + second_total - 2.0 * positive_match)


def on_device(
    embeddings,
    first_weight,
    second_weight,
    bound_index,
    neighbors,
    degree,
    send_index,
    recv_count,
    pair_index,
):
    inputs = embeddings[0]
    row_count, feat_width = inputs.shape
    rim_width = bound_index.shape[-1]
    lower_rows = bound_index[0, 0, 0]
    upper_rows = bound_index[0, 0, 1]
    neighbor_ids = neighbors[0]
    degree_row = degree[0]
    graph_count = lax.axis_size("graph")
    domain_count = lax.axis_size("dom")
    devices = graph_count * domain_count
    routes = send_index[0, 0]
    slot_cap = routes.shape[1]
    pair_count = pair_index.shape[-1]
    adjacency = count_matrix(row_count + 2 * rim_width, neighbor_ids, degree_row)

    def fetch(table):
        edge_rows = jnp.concatenate([table[lower_rows], table[upper_rows]], axis=0)
        extended = with_halo(edge_rows, (("dom", 0),), rim_width)
        return jnp.concatenate([extended[:rim_width], table, extended[-rim_width:]], axis=0)

    def return_rim(grad_pool):
        center = grad_pool[rim_width : rim_width + row_count]
        edge_rows = jnp.concatenate([grad_pool[:rim_width], grad_pool[-rim_width:]], axis=0)
        extended = with_halo(edge_rows, (("dom", 0),), rim_width)
        center = center.at[lower_rows].add(extended[:rim_width])
        return center.at[upper_rows].add(extended[-rim_width:])

    def spread(pool):
        return aggregate(adjacency, pool, degree_row)

    def loss_of(incoming_rows):
        return cluster_term(incoming_rows, recv_count[0, 0], pair_index[0, 0])

    pool_one = fetch(inputs)
    mixed_one, back_one = jax.vjp(spread, pool_one)
    hidden = jnp.tanh(
        jnp.dot(
            mixed_one, first_weight, precision=TOP_PRECISION, preferred_element_type=jnp.float32
        )
    )
    pool_two = fetch(hidden)
    mixed_two, back_two = jax.vjp(spread, pool_two)
    latent = jnp.dot(
        mixed_two, second_weight, precision=TOP_PRECISION, preferred_element_type=jnp.float32
    )
    length = jnp.sqrt(jnp.sum(latent * latent, axis=1, keepdims=True) + EPSILON)
    unit_rows = latent / length
    padded = jnp.concatenate([unit_rows, jnp.zeros((1, feat_width), jnp.float32)], axis=0)
    outgoing = padded[routes]
    arrived = lax.all_to_all(outgoing, ("graph", "dom"), split_axis=0, concat_axis=0, tiled=True)
    arrived = arrived.reshape(devices * slot_cap, feat_width)
    cluster_value, cluster_back = jax.vjp(loss_of, arrived)
    (grad_arrived,) = cluster_back(jnp.ones((), jnp.float32))
    returned = lax.all_to_all(
        grad_arrived.reshape(devices, slot_cap, feat_width),
        ("graph", "dom"),
        split_axis=0,
        concat_axis=0,
        tiled=True,
    )
    grad_unit = (
        jnp.zeros((row_count + 1, feat_width), jnp.float32).at[routes].add(returned)[:row_count]
    )
    grad_latent = (
        grad_unit - unit_rows * jnp.sum(grad_unit * unit_rows, axis=1, keepdims=True)
    ) / length
    grad_second = jnp.dot(
        mixed_two.T, grad_latent, precision=TOP_PRECISION, preferred_element_type=jnp.float32
    )
    grad_mixed_two = jnp.dot(
        grad_latent, second_weight.T, precision=TOP_PRECISION, preferred_element_type=jnp.float32
    )
    (grad_pool_two,) = back_two(grad_mixed_two)
    grad_hidden = return_rim(grad_pool_two)
    grad_inner = grad_hidden * (1.0 - hidden * hidden)
    grad_first = jnp.dot(
        mixed_one.T, grad_inner, precision=TOP_PRECISION, preferred_element_type=jnp.float32
    )
    grad_mixed_one = jnp.dot(
        grad_inner, first_weight.T, precision=TOP_PRECISION, preferred_element_type=jnp.float32
    )
    (grad_pool_one,) = back_one(grad_mixed_one)
    grad_inputs = return_rim(grad_pool_one)
    grad_first, grad_second = lax.psum((grad_first, grad_second), ("graph", "dom"))
    grad_scale = 1.0 / math.sqrt(row_count * devices)
    cluster_mean = (cluster_value / (2.0 * pair_count)).reshape(1, 1)
    return (grad_inputs[None], grad_first * grad_scale, grad_second * grad_scale, cluster_mean)


def solution(mesh):
    in_specs = (
        P("graph", "dom", None),
        P(),
        P(),
        P("graph", "dom", None, None),
        P("graph", "dom", None),
        P("graph", "dom"),
        P("graph", "dom", None, None),
        P("graph", "dom", None),
        P("graph", "dom", None, None),
    )
    out_specs = (P("graph", "dom", None), P(), P(), P("graph", "dom"))
    return jax.shard_map(
        on_device, mesh=mesh, in_specs=in_specs, out_specs=out_specs, check_vma=False
    )
```

profile of v0, /device:TPU:0, one launch (start us, length us, event | category | flops | bytes accessed | tf_op | source)
XLA Modules:
  0.0 331.2 jit_solution(15527398296197626989)
XLA Ops:
  8.5 1.3 copy.44
  10.5 3.0 collective-permute-start
  14.2 4.1 %collective-permute-start.1 = (f32[64,300]{1,0:T(8,128)S(1)}, f32[64,300]{1,0:T(8,128)S(1)}, u32[]{:S(2)}, u32[]{:S(2)}) collective-permute-start(f32[64,300]{1,0:T(8,128)S(1)} %gather_fusion.1), channel_id=1, source_target_pairs={{1,0},{2,1},{3,2},{4,3},{5,4},{6,5},{7,6},{8,7},{9,8},{10,9},{11,1... | collective-permute-start | bytes 230408 | tf_op jit(solution)/shard_map/ppermute | solution.py:21
  18.6 6.2 %convert_reduce_fusion = f32[512,640]{1,0:T(8,128)S(1)} fusion(s32[512,16]{1,0:T(8,128)S(1)} %copy.43, pred[512,16]{1,0:T(8,128)(4,1)S(1)} %iota_compare_fusion.2), kind=kLoop, calls=%fused_computation.13 | loop fusion | flops 20643840 | bytes 1351680 | tf_op jit(solution)/shard_map/reduce_sum | solution.py:35
  24.9 2.2 convolution_divide_fusion.2
  31.0 5.7 %collective-permute-start.3 = (f32[64,300]{0,1:T(8,128)S(1)}, f32[64,300]{0,1:T(8,128)S(1)}, u32[]{:S(2)}, u32[]{:S(2)}) collective-permute-start(f32[64,300]{0,1:T(8,128)S(1)} %copy.48), channel_id=1, source_target_pairs={{1,0},{2,1},{3,2},{4,3},{5,4},{6,5},{7,6},{8,7},{9,8},{10,9},{11,1... | collective-permute-start | bytes 230408 | tf_op jit(solution)/shard_map/ppermute | solution.py:21
  36.7 3.3 collective-permute-done.2
  40.0 2.0 convolution_divide_fusion.3
  44.5 4.8 %gather_fusion.4 = f32[1024,300]{1,0:T(8,128)} fusion(f32[513,300]{1,0:T(8,128)S(1)} %concatenate.17.clone, s32[1024]{0:T(1024)S(1)} %broadcast_clamp_fusion), kind=kCustom, calls=%fused_computation.4 | custom fusion | bytes 2461696 | tf_op jit(solution)/shard_map/gather | solution.py:147
  49.4 5.9 %all-to-all-start = ((f32[32,32,300]{2,1,0:T(8,128)}), f32[32,32,300]{2,1,0:T(8,128)S(1)}, u32[]{:S(2)}, u32[]{:S(2)}) async-start(f32[32,32,300]{2,1,0:T(8,128)} %bitcast.60), calls=%async_computation | async-start | bytes 3145728 | tf_op jit(solution)/shard_map/all_to_all | solution.py:148
  58.0 36.7 %all-to-all-done = f32[32,32,300]{2,1,0:T(8,128)S(1)} async-done(((f32[32,32,300]{2,1,0:T(8,128)}), f32[32,32,300]{2,1,0:T(8,128)S(1)}, u32[]{:S(2)}, u32[]{:S(2)}) %all-to-all-start) | async-done | bytes 1228832 | tf_op jit(solution)/shard_map/all_to_all | solution.py:148
  94.6 1.4 gather_fusion.5
  97.7 1.6 multiply_reduce_fusion.2
  99.3 1.7 copy.51
  105.4 1.4 convolution_add_fusion.1
  107.6 1.4 convolution_add_fusion
  111.2 1.8 copy.52
  113.0 3.1 scatter_fusion
  116.1 41.7 %all_to_all.10 = f32[32,32,300]{2,1,0:T(8,128)} all-to-all(f32[32,32,300]{2,1,0:T(8,128)S(1)} %bitcast.49), channel_id=1, replica_groups=mesh['graph'=2,'dom'=16] {'graph','dom'}, dimensions={0} | all-to-all | bytes 2457600 | tf_op jit(solution)/shard_map/all_to_all | solution.py:152
  157.8 7.7 %scatter_custom_fusion.1 = f32[513,300]{1,0:T(8,128)S(1)} fusion(s32[1024]{0:T(1024)} %copy-done.15, f32[1024,300]{1,0:T(8,128)} %bitcast.61, f32[]{:T(128)} %constant.13.clone.1), kind=kCustom, calls=%fused_computation.50 | custom fusion | flops 307200 | bytes 616112 | tf_op jit(solution)/shard_map/scatter-add | solution.py:160
  166.6 1.4 copy.63
  169.4 2.0 fusion.9
  171.5 5.6 %collective-permute-start.5 = (f32[64,300]{0,1:T(8,128)S(1)}, f32[64,300]{0,1:T(8,128)}, u32[]{:S(2)}, u32[]{:S(2)}) collective-permute-start(f32[64,300]{0,1:T(8,128)S(1)} %get-tuple-element.22), channel_id=1, source_target_pairs={{1,0},{2,1},{3,2},{4,3},{5,4},{6,5},{7,6},{8,7},{9,8},{10,9},{11,1... | collective-permute-start | bytes 230408 | tf_op jit(solution)/shard_map/ppermute | solution.py:21
  177.2 2.0 fusion.54
  181.6 1.3 scatter_fusion.1
  186.3 3.3 fusion.23
  189.6 3.1 convolution_divide_fusion
  193.8 2.0 fusion.8
  196.0 5.6 %collective-permute-start.7 = (f32[64,300]{0,1:T(8,128)S(1)}, f32[64,300]{0,1:T(8,128)S(1)}, u32[]{:S(2)}, u32[]{:S(2)}) collective-permute-start(f32[64,300]{0,1:T(8,128)S(1)} %get-tuple-element.20), channel_id=1, source_target_pairs={{1,0},{2,1},{3,2},{4,3},{5,4},{6,5},{7,6},{8,7},{9,8},{10,9},{11,1... | collective-permute-start | bytes 230408 | tf_op jit(solution)/shard_map/ppermute | solution.py:21
  202.7 2.9 collective-permute-done.6
  209.5 111.5 %all-reduce.6.cloned.1.call-done = (f32[300,300]{1,0:T(8,128)}, f32[300,300]{1,0:T(8,128)}) async-done(((f32[300,300]{1,0:T(8,128)}, f32[300,300]{1,0:T(8,128)}), (f32[300,300]{1,0:T(8,128)}, f32[300,300]{1,0:T(8,128)})) %all-reduce.6.cloned.1.call-update) | async-done | bytes 720016 | tf_op jit(solution)/shard_map/psum | solution.py:182
  321.1 2.1 broadcast_multiply_fusion
  (131 shorter events, 35.0 us)
Async XLA Ops:
  7.2 34.9 %copy-start = (f32[300,300]{1,0:T(8,128)S(1)}, f32[300,300]{1,0:T(8,128)}, u32[]{:S(2)}) copy-start(f32[300,300]{1,0:T(8,128)} %param.11) | copy-start | bytes 1080004
  7.9 6.2 %copy-start.21 = (s32[64]{0:T(128)}, s32[64]{0:T(128)S(1)}, u32[]{:S(2)}) copy-start(s32[64]{0:T(128)S(1)} %get-tuple-element.29) | copy-start | bytes 772
  8.4 9.8 %copy-start.23 = (s32[1,512]{1,0:T(1,128)S(1)}, s32[1,512]{1,0:T(1,128)}, u32[]{:S(2)}) copy-start(s32[1,512]{1,0:T(1,128)} %param.14) | copy-start | bytes 6148
  8.5 9.9 %copy-start.14 = (s32[1,512,16]{1,2,0:T(8,128)S(1)}, s32[1,512,16]{1,2,0:T(8,128)}, u32[]{:S(2)}) copy-start(s32[1,512,16]{1,2,0:T(8,128)} %param.13) | copy-start | bytes 98308
  9.8 8.7 %copy-start.16 = (s32[1,1,32,32]{3,2,1,0:T(8,128)S(1)}, s32[1,1,32,32]{3,2,1,0:T(8,128)}, u32[]{:S(2)}) copy-start(s32[1,1,32,32]{3,2,1,0:T(8,128)} %param.15) | copy-start | bytes 12292
  10.5 14.4 %collective-permute-start = (f32[64,300]{1,0:T(8,128)S(1)}, f32[64,300]{1,0:T(8,128)S(1)}, u32[]{:S(2)}, u32[]{:S(2)}) collective-permute-start(f32[64,300]{1,0:T(8,128)S(1)} %gather_fusion), channel_id=1, source_target_pairs={{0,1},{1,2},{2,3},{3,4},{4,5},{5,6},{6,7},{7,8},{8,9},{9,10},{10,1... | collective-permute-start | bytes 230408 | tf_op jit(solution)/shard_map/ppermute | solution.py:19
  14.2 10.7 %collective-permute-start.1 = (f32[64,300]{1,0:T(8,128)S(1)}, f32[64,300]{1,0:T(8,128)S(1)}, u32[]{:S(2)}, u32[]{:S(2)}) collective-permute-start(f32[64,300]{1,0:T(8,128)S(1)} %gather_fusion.1), channel_id=1, source_target_pairs={{1,0},{2,1},{3,2},{4,3},{5,4},{6,5},{7,6},{8,7},{9,8},{10,9},{11,1... | collective-permute-start | bytes 230408 | tf_op jit(solution)/shard_map/ppermute | solution.py:21
  18.4 21.6 %copy-start.26 = (f32[512]{0:T(512)}, f32[512]{0:T(512)S(1)}, u32[]{:S(2)}) copy-start(f32[512]{0:T(512)S(1)} %convert_add_fusion.5) | copy-start | bytes 6148
  18.6 18.1 %copy-start.15 = (s32[1024]{0:T(1024)}, s32[1024]{0:T(1024)S(1)}, u32[]{:S(2)}) copy-start(s32[1024]{0:T(1024)S(1)} %reshape.282) | copy-start | bytes 12292
  24.8 3.1 copy-start.13
  29.2 10.9 %copy-start.3 = (f32[512,300]{0,1:T(8,128)}, f32[512,300]{0,1:T(8,128)S(1)}, u32[]{:S(2)}) copy-start(f32[512,300]{0,1:T(8,128)S(1)} %convolution_tanh_fusion) | copy-start | bytes 1843204
  30.9 9.1 %collective-permute-start.2 = (f32[64,300]{0,1:T(8,128)S(1)}, f32[64,300]{0,1:T(8,128)S(1)}, u32[]{:S(2)}, u32[]{:S(2)}) collective-permute-start(f32[64,300]{0,1:T(8,128)S(1)} %copy.46), channel_id=1, source_target_pairs={{0,1},{1,2},{2,3},{3,4},{4,5},{5,6},{6,7},{7,8},{8,9},{9,10},{10,1... | collective-permute-start | bytes 230408 | tf_op jit(solution)/shard_map/ppermute | solution.py:19
  31.0 9.0 %collective-permute-start.3 = (f32[64,300]{0,1:T(8,128)S(1)}, f32[64,300]{0,1:T(8,128)S(1)}, u32[]{:S(2)}, u32[]{:S(2)}) collective-permute-start(f32[64,300]{0,1:T(8,128)S(1)} %copy.48), channel_id=1, source_target_pairs={{1,0},{2,1},{3,2},{4,3},{5,4},{6,5},{7,6},{8,7},{9,8},{10,9},{11,1... | collective-permute-start | bytes 230408 | tf_op jit(solution)/shard_map/ppermute | solution.py:21
  49.4 6.1 %copy-start.29 = (s32[1,1,32]{2,1,0:T(1,128)S(1)}, s32[1,1,32]{2,1,0:T(1,128)}, u32[]{:S(2)}) copy-start(s32[1,1,32]{2,1,0:T(1,128)} %param.16) | copy-start | bytes 388
  49.4 7.4 %copy-start.28 = (s32[1,1,2,128]{3,2,1,0:T(2,128)S(1)}, s32[1,1,2,128]{3,2,1,0:T(2,128)}, u32[]{:S(2)}) copy-start(s32[1,1,2,128]{3,2,1,0:T(2,128)} %param.17) | copy-start | bytes 3076
  49.4 45.2 %all-to-all-start = ((f32[32,32,300]{2,1,0:T(8,128)}), f32[32,32,300]{2,1,0:T(8,128)S(1)}, u32[]{:S(2)}, u32[]{:S(2)}) async-start(f32[32,32,300]{2,1,0:T(8,128)} %bitcast.60), calls=%async_computation | async-start | bytes 3145728 | tf_op jit(solution)/shard_map/all_to_all | solution.py:148
  55.3 265.8 %all-reduce.6.cloned.1.call-start = ((), (), s32[]{:S(2)}) async-start(), calls=%async_computation.2 | async-start | bytes 1867776 | tf_op jit(solution)/shard_map/psum | solution.py:182
  101.0 1.9 copy-start.17
  101.1 2.8 copy-start.25
  103.0 2.4 copy-start.12
  105.4 2.2 copy-start.11
  111.2 1.8 copy-start.24
  165.6 2.4 copy-start.2
  169.4 7.8 %copy-start.9 = (f32[512,300]{0,1:T(8,128)S(1)}, f32[512,300]{0,1:T(8,128)}, u32[]{:S(2)}) copy-start(f32[512,300]{0,1:T(8,128)} %copy-done.8) | copy-start | bytes 1843204
  171.5 9.1 %collective-permute-start.4 = (f32[64,300]{0,1:T(8,128)S(1)}, f32[64,300]{0,1:T(8,128)}, u32[]{:S(2)}, u32[]{:S(2)}) collective-permute-start(f32[64,300]{0,1:T(8,128)S(1)} %get-tuple-element.23), channel_id=1, source_target_pairs={{0,1},{1,2},{2,3},{3,4},{4,5},{5,6},{6,7},{7,8},{8,9},{9,10},{10,1... | collective-permute-start | bytes 230408 | tf_op jit(solution)/shard_map/ppermute | solution.py:19
  171.5 11.4 %collective-permute-start.5 = (f32[64,300]{0,1:T(8,128)S(1)}, f32[64,300]{0,1:T(8,128)}, u32[]{:S(2)}, u32[]{:S(2)}) collective-permute-start(f32[64,300]{0,1:T(8,128)S(1)} %get-tuple-element.22), channel_id=1, source_target_pairs={{1,0},{2,1},{3,2},{4,3},{5,4},{6,5},{7,6},{8,7},{9,8},{10,9},{11,1... | collective-permute-start | bytes 230408 | tf_op jit(solution)/shard_map/ppermute | solution.py:21
  179.2 2.5 copy-start.22
  179.7 4.3 %copy-start.20 = (s32[64]{0:T(128)S(1)}, s32[64]{0:T(128)}, u32[]{:S(2)}) copy-start(s32[64]{0:T(128)} %copy-done.19) | copy-start | bytes 772
  184.0 2.4 copy-start.4
  186.3 3.3 copy-start.6
  195.9 9.7 %collective-permute-start.6 = (f32[64,300]{0,1:T(8,128)S(1)}, f32[64,300]{0,1:T(8,128)S(1)}, u32[]{:S(2)}, u32[]{:S(2)}) collective-permute-start(f32[64,300]{0,1:T(8,128)S(1)} %get-tuple-element.21), channel_id=1, source_target_pairs={{0,1},{1,2},{2,3},{3,4},{4,5},{5,6},{6,7},{7,8},{8,9},{9,10},{10,1... | collective-permute-start | bytes 230408 | tf_op jit(solution)/shard_map/ppermute | solution.py:19
  196.0 11.0 %collective-permute-start.7 = (f32[64,300]{0,1:T(8,128)S(1)}, f32[64,300]{0,1:T(8,128)S(1)}, u32[]{:S(2)}, u32[]{:S(2)}) collective-permute-start(f32[64,300]{0,1:T(8,128)S(1)} %get-tuple-element.20), channel_id=1, source_target_pairs={{1,0},{2,1},{3,2},{4,3},{5,4},{6,5},{7,6},{8,7},{9,8},{10,9},{11,1... | collective-permute-start | bytes 230408 | tf_op jit(solution)/shard_map/ppermute | solution.py:21
  (8 other events, 7.9 us)
Sparse Core Ops, SparseCore 0:
  192.9 128.1 all-reduce.5
where the time goes:
time: 332 us; the launch traced here: 331 us
  waiting for transfers between devices  155 us (47%)
  blocking collectives  41.7 us (13%)
  local copies, waits for them, and re-layouts  30.7 us (9%)
  starting transfers between devices  30.2 us (9%)
  other arithmetic  30.1 us (9%)
  matrix products  26.7 us (8%)
  between operations  16.4 us (5%)
    psum x1, waiting for transfers between devices, on_device(): lax.psum((grad_first, grad_second), ('graph', 'dom'))  112 us
    all_to_all x1, blocking collectives, on_device(): lax.all_to_all(grad_arrived.reshape(devices, slot_cap, feat_width), ('gra...  41.7 us
    all_to_all x1, waiting for transfers between devices, on_device(): lax.all_to_all(outgoing, ('graph', 'dom'), split_axis=0, concat_axis=0, t...  36.7 us
    ppermute x4, starting transfers between devices, with_halo(): lax.ppermute(head, axis, [((i + 1) % count, i) for i in range(count)])  20.9 us
    unnamed x64, local copies, waits for them, and re-layouts  8.23 us
    dot_general x4, matrix products, aggregate(): jnp.dot(counts, pool, precision=TOP_PRECISION, preferred_element_type=jnp...  8.09 us
    scatter-add x1, other arithmetic, on_device(): jnp.zeros((row_count + 1, feat_width), jnp.float32).at[routes].add(returned)  7.75 us
    ppermute x4, waiting for transfers between devices, with_halo(): lax.ppermute(tail, axis, [(i, (i + 1) % count) for i in range(count)])  7.12 us
  transfers between devices with their start and end apart: 10, of which 5 were waited for; matrix products, arithmetic and copies ran while one was open for 6% of the time, Pallas kernels for 0%

commit v1 on v0

--- a/solution.py
+++ b/solution.py
@@ -179,7 +179,7 @@
     )
     (grad_pool_one,) = back_one(grad_mixed_one)
     grad_inputs = return_rim(grad_pool_one)
-    grad_first, grad_second = lax.psum((grad_first, grad_second), ("graph", "dom"))
+    grad_first, grad_second = lax.psum(lax.psum((grad_first, grad_second), "dom"), "graph")
     grad_scale = 1.0 / math.sqrt(row_count * devices)
     cluster_mean = (cluster_value / (2.0 * pair_count)).reshape(1, 1)
     return (grad_inputs[None], grad_first * grad_scale, grad_second * grad_scale, cluster_mean)

time: 332 us -> 332 us (level)
    psum x1 -> x2, waiting for transfers between devices: 112 us -> 115 us  [the longest x1 110 us: on_device(): lax.psum((grad_first, grad_second), 'dom')]
  transfers between devices with their start and end apart: 10 -> 11, of which waited for: 5 -> 6; matrix products, arithmetic and copies ran while one was open for 6% -> 7% of each run, Pallas kernels for 0% -> 0%
where the time goes in v1:
time: 332 us; the launch traced here: 331 us
  waiting for transfers between devices  158 us (48%)
  blocking collectives  41.7 us (13%)
  starting transfers between devices  30.3 us (9%)
  other arithmetic  30.1 us (9%)
  local copies, waits for them, and re-layouts  29.6 us (9%)
  matrix products  24.8 us (7%)
  between operations  16.5 us (5%)
    psum x1, waiting for transfers between devices, on_device(): lax.psum((grad_first, grad_second), 'dom')  110 us
    all_to_all x1, blocking collectives, on_device(): lax.all_to_all(grad_arrived.reshape(devices, slot_cap, feat_width), ('gra...  41.7 us
    all_to_all x1, waiting for transfers between devices, on_device(): lax.all_to_all(outgoing, ('graph', 'dom'), split_axis=0, concat_axis=0, t...  36.6 us
    ppermute x4, starting transfers between devices, with_halo(): lax.ppermute(head, axis, [((i + 1) % count, i) for i in range(count)])  19.5 us
    dot_general x4, matrix products, aggregate(): jnp.dot(counts, pool, precision=TOP_PRECISION, preferred_element_type=jnp...  8.11 us
    scatter-add x1, other arithmetic, on_device(): jnp.zeros((row_count + 1, feat_width), jnp.float32).at[routes].add(returned)  7.75 us
    unnamed x64, local copies, waits for them, and re-layouts  7.18 us
  transfers between devices with their start and end apart: 11, of which 6 were waited for; matrix products, arithmetic and copies ran while one was open for 7% of the time, Pallas kernels for 0%

profile of v1, /device:TPU:0, one launch (start us, length us, event | category | flops | bytes accessed | tf_op | source)
XLA Modules:
  0.0 331.2 jit_solution(7884964884649592256)
XLA Ops:
  8.5 1.3 copy.44
  10.5 3.0 collective-permute-start
  14.2 4.1 %collective-permute-start.1 = (f32[64,300]{1,0:T(8,128)S(1)}, f32[64,300]{1,0:T(8,128)S(1)}, u32[]{:S(2)}, u32[]{:S(2)}) collective-permute-start(f32[64,300]{1,0:T(8,128)S(1)} %gather_fusion.1), channel_id=1, source_target_pairs={{1,0},{2,1},{3,2},{4,3},{5,4},{6,5},{7,6},{8,7},{9,8},{10,9},{11,1... | collective-permute-start | bytes 230408 | tf_op jit(solution)/shard_map/ppermute | solution.py:21
  18.6 6.2 %convert_reduce_fusion = f32[512,640]{1,0:T(8,128)S(1)} fusion(s32[512,16]{1,0:T(8,128)S(1)} %copy.43, pred[512,16]{1,0:T(8,128)(4,1)S(1)} %iota_compare_fusion.2), kind=kLoop, calls=%fused_computation.13 | loop fusion | flops 20643840 | bytes 1351680 | tf_op jit(solution)/shard_map/reduce_sum | solution.py:35
  24.9 2.2 convolution_divide_fusion.2
  31.1 5.7 %collective-permute-start.3 = (f32[64,300]{0,1:T(8,128)S(1)}, f32[64,300]{0,1:T(8,128)S(1)}, u32[]{:S(2)}, u32[]{:S(2)}) collective-permute-start(f32[64,300]{0,1:T(8,128)S(1)} %copy.48), channel_id=1, source_target_pairs={{1,0},{2,1},{3,2},{4,3},{5,4},{6,5},{7,6},{8,7},{9,8},{10,9},{11,1... | collective-permute-start | bytes 230408 | tf_op jit(solution)/shard_map/ppermute | solution.py:21
  36.7 3.3 collective-permute-done.2
  40.0 2.0 convolution_divide_fusion.3
  44.5 4.8 %gather_fusion.4 = f32[1024,300]{1,0:T(8,128)} fusion(f32[513,300]{1,0:T(8,128)S(1)} %concatenate.17.clone, s32[1024]{0:T(1024)S(1)} %broadcast_clamp_fusion), kind=kCustom, calls=%fused_computation.4 | custom fusion | bytes 2461696 | tf_op jit(solution)/shard_map/gather | solution.py:147
  49.3 5.9 %all-to-all-start = ((f32[32,32,300]{2,1,0:T(8,128)}), f32[32,32,300]{2,1,0:T(8,128)S(1)}, u32[]{:S(2)}, u32[]{:S(2)}) async-start(f32[32,32,300]{2,1,0:T(8,128)} %bitcast.60), calls=%async_computation | async-start | bytes 3145728 | tf_op jit(solution)/shard_map/all_to_all | solution.py:148
  58.0 36.6 %all-to-all-done = f32[32,32,300]{2,1,0:T(8,128)S(1)} async-done(((f32[32,32,300]{2,1,0:T(8,128)}), f32[32,32,300]{2,1,0:T(8,128)S(1)}, u32[]{:S(2)}, u32[]{:S(2)}) %all-to-all-start) | async-done | bytes 1228832 | tf_op jit(solution)/shard_map/all_to_all | solution.py:148
  94.6 1.4 gather_fusion.5
  97.7 1.6 multiply_reduce_fusion.2
  99.3 1.7 copy.51
  105.3 1.4 convolution_add_fusion.1
  107.6 1.4 convolution_add_fusion
  111.1 1.8 copy.52
  112.9 3.1 scatter_fusion
  116.1 41.7 %all_to_all.10 = f32[32,32,300]{2,1,0:T(8,128)} all-to-all(f32[32,32,300]{2,1,0:T(8,128)S(1)} %bitcast.49), channel_id=1, replica_groups=mesh['graph'=2,'dom'=16] {'graph','dom'}, dimensions={0} | all-to-all | bytes 2457600 | tf_op jit(solution)/shard_map/all_to_all | solution.py:152
  157.8 7.7 %scatter_custom_fusion.1 = f32[513,300]{1,0:T(8,128)S(1)} fusion(s32[1024]{0:T(1024)} %copy-done.15, f32[1024,300]{1,0:T(8,128)} %bitcast.61, f32[]{:T(128)} %constant.13.clone.1), kind=kCustom, calls=%fused_computation.50 | custom fusion | flops 307200 | bytes 616112 | tf_op jit(solution)/shard_map/scatter-add | solution.py:160
  166.5 1.4 copy.63
  169.3 2.0 fusion.9
  171.5 5.6 %collective-permute-start.5 = (f32[64,300]{0,1:T(8,128)S(1)}, f32[64,300]{0,1:T(8,128)}, u32[]{:S(2)}, u32[]{:S(2)}) collective-permute-start(f32[64,300]{0,1:T(8,128)S(1)} %get-tuple-element.24), channel_id=1, source_target_pairs={{1,0},{2,1},{3,2},{4,3},{5,4},{6,5},{7,6},{8,7},{9,8},{10,9},{11,1... | collective-permute-start | bytes 230408 | tf_op jit(solution)/shard_map/ppermute | solution.py:21
  177.1 2.0 fusion.54
  186.3 3.2 fusion.23
  189.6 110.2 %all-reduce.8.cloned.1.call-done = (f32[300,300]{1,0:T(8,128)}, f32[300,300]{1,0:T(8,128)}) async-done(((f32[300,300]{1,0:T(8,128)}, f32[300,300]{1,0:T(8,128)}), (f32[300,300]{1,0:T(8,128)}, f32[300,300]{1,0:T(8,128)})) %all-reduce.8.cloned.1.call-update) | async-done | bytes 720016 | tf_op jit(solution)/shard_map/psum | solution.py:182
  301.1 2.0 fusion.8
  303.2 1.5 collective-permute-start.6
  304.6 4.2 %collective-permute-start.7 = (f32[64,300]{0,1:T(8,128)S(1)}, f32[64,300]{0,1:T(8,128)S(1)}, u32[]{:S(2)}, u32[]{:S(2)}) collective-permute-start(f32[64,300]{0,1:T(8,128)S(1)} %get-tuple-element.22), channel_id=1, source_target_pairs={{1,0},{2,1},{3,2},{4,3},{5,4},{6,5},{7,6},{8,7},{9,8},{10,9},{11,1... | collective-permute-start | bytes 230408 | tf_op jit(solution)/shard_map/ppermute | solution.py:21
  310.0 2.2 collective-permute-done.6
  316.1 5.0 %all-reduce.10.cloned.1.call-done = (f32[300,300]{1,0:T(8,128)}, f32[300,300]{1,0:T(8,128)}) async-done(((f32[300,300]{1,0:T(8,128)}, f32[300,300]{1,0:T(8,128)}), (f32[300,300]{1,0:T(8,128)}, f32[300,300]{1,0:T(8,128)})) %all-reduce.10.cloned.1.call-update) | async-done | bytes 720016 | tf_op jit(solution)/shard_map/psum | solution.py:182
  321.0 2.1 broadcast_multiply_fusion
  (134 shorter events, 36.5 us)
Async XLA Ops:
  7.2 34.9 %copy-start = (f32[300,300]{1,0:T(8,128)S(1)}, f32[300,300]{1,0:T(8,128)}, u32[]{:S(2)}) copy-start(f32[300,300]{1,0:T(8,128)} %param.11) | copy-start | bytes 1080004
  7.9 6.2 %copy-start.21 = (s32[64]{0:T(128)}, s32[64]{0:T(128)S(1)}, u32[]{:S(2)}) copy-start(s32[64]{0:T(128)S(1)} %get-tuple-element.31) | copy-start | bytes 772
  8.5 9.8 %copy-start.23 = (s32[1,512]{1,0:T(1,128)S(1)}, s32[1,512]{1,0:T(1,128)}, u32[]{:S(2)}) copy-start(s32[1,512]{1,0:T(1,128)} %param.14) | copy-start | bytes 6148
  8.5 9.9 %copy-start.14 = (s32[1,512,16]{1,2,0:T(8,128)S(1)}, s32[1,512,16]{1,2,0:T(8,128)}, u32[]{:S(2)}) copy-start(s32[1,512,16]{1,2,0:T(8,128)} %param.13) | copy-start | bytes 98308
  9.8 8.7 %copy-start.16 = (s32[1,1,32,32]{3,2,1,0:T(8,128)S(1)}, s32[1,1,32,32]{3,2,1,0:T(8,128)}, u32[]{:S(2)}) copy-start(s32[1,1,32,32]{3,2,1,0:T(8,128)} %param.15) | copy-start | bytes 12292
  10.5 14.4 %collective-permute-start = (f32[64,300]{1,0:T(8,128)S(1)}, f32[64,300]{1,0:T(8,128)S(1)}, u32[]{:S(2)}, u32[]{:S(2)}) collective-permute-start(f32[64,300]{1,0:T(8,128)S(1)} %gather_fusion), channel_id=1, source_target_pairs={{0,1},{1,2},{2,3},{3,4},{4,5},{5,6},{6,7},{7,8},{8,9},{9,10},{10,1... | collective-permute-start | bytes 230408 | tf_op jit(solution)/shard_map/ppermute | solution.py:19
  14.2 10.7 %collective-permute-start.1 = (f32[64,300]{1,0:T(8,128)S(1)}, f32[64,300]{1,0:T(8,128)S(1)}, u32[]{:S(2)}, u32[]{:S(2)}) collective-permute-start(f32[64,300]{1,0:T(8,128)S(1)} %gather_fusion.1), channel_id=1, source_target_pairs={{1,0},{2,1},{3,2},{4,3},{5,4},{6,5},{7,6},{8,7},{9,8},{10,9},{11,1... | collective-permute-start | bytes 230408 | tf_op jit(solution)/shard_map/ppermute | solution.py:21
  18.4 21.6 %copy-start.26 = (f32[512]{0:T(512)}, f32[512]{0:T(512)S(1)}, u32[]{:S(2)}) copy-start(f32[512]{0:T(512)S(1)} %convert_add_fusion.5) | copy-start | bytes 6148
  18.6 18.1 %copy-start.15 = (s32[1024]{0:T(1024)}, s32[1024]{0:T(1024)S(1)}, u32[]{:S(2)}) copy-start(s32[1024]{0:T(1024)S(1)} %reshape.282) | copy-start | bytes 12292
  24.8 3.1 copy-start.12
  29.2 10.8 %copy-start.3 = (f32[512,300]{0,1:T(8,128)}, f32[512,300]{0,1:T(8,128)S(1)}, u32[]{:S(2)}) copy-start(f32[512,300]{0,1:T(8,128)S(1)} %convolution_tanh_fusion) | copy-start | bytes 1843204
  30.9 9.1 %collective-permute-start.2 = (f32[64,300]{0,1:T(8,128)S(1)}, f32[64,300]{0,1:T(8,128)S(1)}, u32[]{:S(2)}, u32[]{:S(2)}) collective-permute-start(f32[64,300]{0,1:T(8,128)S(1)} %copy.46), channel_id=1, source_target_pairs={{0,1},{1,2},{2,3},{3,4},{4,5},{5,6},{6,7},{7,8},{8,9},{9,10},{10,1... | collective-permute-start | bytes 230408 | tf_op jit(solution)/shard_map/ppermute | solution.py:19
  31.1 9.0 %collective-permute-start.3 = (f32[64,300]{0,1:T(8,128)S(1)}, f32[64,300]{0,1:T(8,128)S(1)}, u32[]{:S(2)}, u32[]{:S(2)}) collective-permute-start(f32[64,300]{0,1:T(8,128)S(1)} %copy.48), channel_id=1, source_target_pairs={{1,0},{2,1},{3,2},{4,3},{5,4},{6,5},{7,6},{8,7},{9,8},{10,9},{11,1... | collective-permute-start | bytes 230408 | tf_op jit(solution)/shard_map/ppermute | solution.py:21
  49.3 6.1 %copy-start.29 = (s32[1,1,32]{2,1,0:T(1,128)S(1)}, s32[1,1,32]{2,1,0:T(1,128)}, u32[]{:S(2)}) copy-start(s32[1,1,32]{2,1,0:T(1,128)} %param.16) | copy-start | bytes 388
  49.3 7.5 %copy-start.28 = (s32[1,1,2,128]{3,2,1,0:T(2,128)S(1)}, s32[1,1,2,128]{3,2,1,0:T(2,128)}, u32[]{:S(2)}) copy-start(s32[1,1,2,128]{3,2,1,0:T(2,128)} %param.17) | copy-start | bytes 3076
  49.3 45.2 %all-to-all-start = ((f32[32,32,300]{2,1,0:T(8,128)}), f32[32,32,300]{2,1,0:T(8,128)S(1)}, u32[]{:S(2)}, u32[]{:S(2)}) async-start(f32[32,32,300]{2,1,0:T(8,128)} %bitcast.60), calls=%async_computation | async-start | bytes 3145728 | tf_op jit(solution)/shard_map/all_to_all | solution.py:148
  55.2 244.5 %all-reduce.8.cloned.1.call-start = ((), (), s32[]{:S(2)}) async-start(), calls=%async_computation.2 | async-start | bytes 1867776 | tf_op jit(solution)/shard_map/psum | solution.py:182
  101.1 2.9 copy-start.25
  102.9 2.4 copy-start.11
  105.3 2.2 copy-start.10
  165.5 2.4 copy-start.2
  169.3 7.8 %copy-start.9 = (f32[512,300]{0,1:T(8,128)S(1)}, f32[512,300]{0,1:T(8,128)}, u32[]{:S(2)}) copy-start(f32[512,300]{0,1:T(8,128)} %copy-done.8) | copy-start | bytes 1843204
  171.4 9.1 %collective-permute-start.4 = (f32[64,300]{0,1:T(8,128)S(1)}, f32[64,300]{0,1:T(8,128)}, u32[]{:S(2)}, u32[]{:S(2)}) collective-permute-start(f32[64,300]{0,1:T(8,128)S(1)} %get-tuple-element.25), channel_id=1, source_target_pairs={{0,1},{1,2},{2,3},{3,4},{4,5},{5,6},{6,7},{7,8},{8,9},{9,10},{10,1... | collective-permute-start | bytes 230408 | tf_op jit(solution)/shard_map/ppermute | solution.py:19
  171.5 11.4 %collective-permute-start.5 = (f32[64,300]{0,1:T(8,128)S(1)}, f32[64,300]{0,1:T(8,128)}, u32[]{:S(2)}, u32[]{:S(2)}) collective-permute-start(f32[64,300]{0,1:T(8,128)S(1)} %get-tuple-element.24), channel_id=1, source_target_pairs={{1,0},{2,1},{3,2},{4,3},{5,4},{6,5},{7,6},{8,7},{9,8},{10,9},{11,1... | collective-permute-start | bytes 230408 | tf_op jit(solution)/shard_map/ppermute | solution.py:21
  179.1 2.5 copy-start.22
  179.6 4.3 %copy-start.20 = (s32[64]{0:T(128)S(1)}, s32[64]{0:T(128)}, u32[]{:S(2)}) copy-start(s32[64]{0:T(128)} %copy-done.19) | copy-start | bytes 772
  183.9 2.4 copy-start.4
  189.5 110.3 %copy-start.6 = (f32[512,300]{0,1:T(8,128)S(1)}, f32[512,300]{0,1:T(8,128)}, u32[]{:S(2)}) copy-start(f32[512,300]{0,1:T(8,128)} %copy.58) | copy-start | bytes 1843204
  189.5 110.3 %copy-start.13 = (f32[300,300]{1,0:T(8,128)S(1)}, f32[300,300]{1,0:T(8,128)}, u32[]{:S(2)}) copy-start(f32[300,300]{1,0:T(8,128)} %param.10) | copy-start | bytes 1080004
  189.5 131.5 %all-reduce.10.cloned.1.call-start = ((), (), s32[]{:S(2)}) async-start(), calls=%async_computation.3 | async-start | bytes 1867776 | tf_op jit(solution)/shard_map/psum | solution.py:182
  303.2 9.0 %collective-permute-start.6 = (f32[64,300]{0,1:T(8,128)S(1)}, f32[64,300]{0,1:T(8,128)S(1)}, u32[]{:S(2)}, u32[]{:S(2)}) collective-permute-start(f32[64,300]{0,1:T(8,128)S(1)} %get-tuple-element.23), channel_id=1, source_target_pairs={{0,1},{1,2},{2,3},{3,4},{4,5},{5,6},{6,7},{7,8},{8,9},{9,10},{10,1... | collective-permute-start | bytes 230408 | tf_op jit(solution)/shard_map/ppermute | solution.py:19
  304.6 8.9 %collective-permute-start.7 = (f32[64,300]{0,1:T(8,128)S(1)}, f32[64,300]{0,1:T(8,128)S(1)}, u32[]{:S(2)}, u32[]{:S(2)}) collective-permute-start(f32[64,300]{0,1:T(8,128)S(1)} %get-tuple-element.22), channel_id=1, source_target_pairs={{1,0},{2,1},{3,2},{4,3},{5,4},{6,5},{7,6},{8,7},{9,8},{10,9},{11,1... | collective-permute-start | bytes 230408 | tf_op jit(solution)/shard_map/ppermute | solution.py:21
  (9 other events, 10.6 us)
Sparse Core Ops, SparseCore 0:
  189.7 110.0 all-reduce.7
  302.1 18.8 all-reduce.9
